TPU v7x, 128 devices: a whole 4x4x4 slice. The times are simulated.
128 devices in a mesh: scene: 8 (over y, core), frame: 16 (over z, x).
Axes of the slice: x: 4, y: 4, z: 4, core: 2. Of those that a mesh axis runs over, the one named last changes fastest.
Arguments:
- occupancy: bfloat16 [8, 64, 64, 2048], P('scene', 'frame'), may hold values from -6 to 6
- scene_lengths: int32 [8], P('scene'), may hold values from 8 to 64, as said below
- conv1_weight: bfloat16 [128, 1728], replicated, may hold values from -0.15625 to 0.15625
- conv2_weight: bfloat16 [256, 3456], replicated, may hold values from -0.109375 to 0.109375
- temporal_weight: bfloat16 [3, 256, 256], replicated, may hold values from -0.21875 to 0.21875
- query_weight: bfloat16 [256, 256], replicated
- key_weight: bfloat16 [256, 256], replicated
- value_weight: bfloat16 [256, 256], replicated, may hold values from -0.375 to 0.375
- out_weight: bfloat16 [256, 256], replicated, may hold values from -0.375 to 0.375
Outputs:
- encoded: bfloat16 [8, 64, 256, 512], P('scene', 'frame')
- kl_loss: float32 [], replicated
Inputs may be any that keep to these rules, and one draw needn't show every extreme that they name: `scene_lengths`: non-decreasing along the scenes; the first scene has exactly 8 frames with data and the last exactly 64.
All inputs are finite; a program needn't handle non-finite values.
Results may differ from a plain program's by a relative error of at most 0.011.
Values may be sent and summed in bfloat16 or wider, within the bound.
A program may use at most 192 MiB of HBM per device.

v0:
```python
import jax
import jax.numpy as jnp
from jax import lax
from jax.sharding import PartitionSpec as P

CIN = 64
C1 = 128
C2 = 256
HEADS = 4
HD = 64
HI = 16
ZD = 8
CELLS = 512
NORM_EPS = 1e-06


def spatial_conv(voxels, weight, channels_in, stride):
    channels_out = weight.shape[0]
    kernel = weight.reshape(channels_out, channels_in, 3, 3, 3)
    return lax.conv_general_dilated(
        voxels,
        kernel,
        (stride, stride, 1),
        ((1, 1), (1, 1), (1, 1)),
        dimension_numbers=("NCDHW", "OIDHW", "NCDHW"),
        preferred_element_type=jnp.float32,
    )


def mix(maps, weight):
    return jnp.einsum("tnc,oc->tno", maps, weight, preferred_element_type=jnp.float32)


def shards(
    occupancy,
    scene_lengths,
    conv1_weight,
    conv2_weight,
    temporal_weight,
    query_weight,
    key_weight,
    value_weight,
    out_weight,
):
    f_dev = occupancy.shape[1]
    length = scene_lengths[0]
    first_frame = lax.axis_index("frame") * f_dev
    frame_ids = first_frame + jnp.arange(f_dev, dtype=jnp.int32)
    valid_rows = (frame_ids < length).astype(jnp.float32)
    voxels = occupancy[0].reshape(f_dev, CIN, HI, HI, ZD)
    first_maps = jax.nn.silu(spatial_conv(voxels, conv1_weight, CIN, 2)).astype(jnp.bfloat16)
    second_full = jax.nn.silu(spatial_conv(first_maps, conv2_weight, C1, 1))
    second_maps = (second_full.reshape(f_dev, C2, CELLS) * valid_rows[:, None, None]).astype(
        jnp.bfloat16
    )
    second = lax.all_to_all(second_maps.transpose(0, 2, 1), "frame", 1, 0, tiled=True)
    frames, cells = second.shape[:2]
    padded = jnp.pad(second, ((1, 1), (0, 0), (0, 0)))
    temporal_sum = mix(padded[0:frames], temporal_weight[0])
    for tap in range(1, 3):
        temporal_sum = temporal_sum + mix(padded[tap : tap + frames], temporal_weight[tap])
    residual = (second.astype(jnp.float32) + jax.nn.silu(temporal_sum)).astype(jnp.bfloat16)
    residual = residual.astype(jnp.float32)
    normed = (
        residual * lax.rsqrt(jnp.mean(residual * residual, axis=2, keepdims=True) + NORM_EPS)
    ).astype(jnp.bfloat16)
    split = (frames, cells, HEADS, HD)
    queries = mix(normed, query_weight).astype(jnp.bfloat16).reshape(split)
    keys = mix(normed, key_weight).astype(jnp.bfloat16).reshape(split)
    values = mix(normed, value_weight).astype(jnp.bfloat16).reshape(split)
    scores = jnp.einsum(
        "qnhd,knhd->nhqk", queries, keys, preferred_element_type=jnp.float32
    ) * HD ** (-0.5)
    key_mask = (jnp.arange(frames) < length)[None, None, None, :]
    scores = jnp.where(key_mask, scores, -1e30)
    row_max = jnp.max(scores, axis=3, keepdims=True)
    weights = jnp.where(key_mask, jnp.exp(scores - row_max), 0.0)
    total = jnp.sum(weights, axis=3, keepdims=True)
    weighted = jnp.einsum(
        "nhqk,knhd->nhqd", weights.astype(jnp.bfloat16), values, preferred_element_type=jnp.float32
    )
    attended = (weighted / total).astype(jnp.bfloat16)
    attended = attended.transpose(2, 0, 1, 3).reshape(frames, cells, C2)
    row_valid = (jnp.arange(frames) < length).astype(jnp.float32)[:, None, None]
    encoded = ((residual + mix(attended, out_weight)) * row_valid).astype(jnp.bfloat16)
    squares = jnp.sum(jnp.square(encoded.astype(jnp.float32)))
    grand_total = lax.psum(squares, ("scene", "frame"))
    slot_count = float(lax.axis_size("scene") * frames * CELLS * C2)
    kl_loss = 0.5 * grand_total / slot_count
    encoded = lax.all_to_all(encoded, "frame", 0, 1, tiled=True).transpose(0, 2, 1)
    return (encoded[None], kl_loss)


def solution(mesh):
    placed = (P("scene", "frame", None, None), P("scene"), P(), P(), P(), P(), P(), P(), P())
    return jax.shard_map(
        shards,
        mesh=mesh,
        in_specs=placed,
        out_specs=(P("scene", "frame", None, None), P()),
        check_vma=False,
    )
```

profile of v0, /device:TPU:1, one launch (start us, length us, event | category | flops | bytes accessed | tf_op | source)
XLA Modules:
  0.0 162.8 jit_solution(13435538620634952501)
XLA Ops:
  0.6 0.0 copy-start
  1.3 2.6 %copy.23 = bf16[256,3456]{0,1:T(8,128)(2,1)S(1)} copy(bf16[256,3456]{1,0:T(8,128)(2,1)} %param.12) | data formatting | bytes 3538944 | tf_op args[3]
  4.0 0.0 copy-start.3
  4.0 2.9 %reshape.51 = bf16[256,128,3,3,3]{0,4,3,2,1:T(4,128)(2,1)} reshape(bf16[256,3456]{0,1:T(8,128)(2,1)S(1)} %copy.23) | data formatting | bytes 3538944 | tf_op jit(solution)/shard_map/reshape | solution.py:19
  6.8 0.0 copy-done.3
  6.8 1.1 copy.20
  7.9 1.5 reshape.50
  9.4 0.0 copy-start.1
  9.4 5.0 %fusion.22 = bf16[4,128,8,8,8]{1,0,4,3,2:T(4,128)(2,1)S(1)} fusion(bf16[4,64,16,16,8]{1,4,3,2,0:T(8,128)(2,1)S(1)} %bitcast.70, bf16[128,64,3,3,3]{0,4,3,2,1:T(4,128)(2,1)S(1)} %reshape.50), kind=kOutput, calls=%fused_computation.34 | convolution fusion | flops 764018688 | bytes 2015232 | tf_op jit(solution)/shard_map/conv_general_dilated | solution.py:20
  14.4 0.0 copy-done.1
  14.4 6.6 %divide_multiply_fusion = f32[4,256,8,8,8]{1,0,4,3,2:T(4,128)S(1)} fusion(bf16[4,128,8,8,8]{1,0,4,3,2:T(4,128)(2,1)S(1)} %fusion.22, bf16[256,128,3,3,3]{0,4,3,2,1:T(4,128)(2,1)S(1)} %copy-done.1), kind=kOutput, calls=%fused_computation.9 | convolution fusion | flops 2793406464 | bytes 4390912 | tf_op jit(solution)/shard_map/conv_general_dilated | solution.py:20
  21.0 1.5 fusion.7
  22.6 0.0 copy-start.4
  22.6 8.6 %all-to-all-start = ((bf16[4,512,256]{2,0,1:T(4,128)(2,1)}), bf16[4,512,256]{2,0,1:T(4,128)(2,1)S(1)}, u32[]{:S(2)}, u32[]{:S(2)}) async-start(bf16[4,512,256]{2,0,1:T(4,128)(2,1)} %bitcast.3), calls=%async_computation | async-start | bytes 2097152 | tf_op jit(solution)/shard_map/all_to_all | solution.py:56
  31.2 16.0 %all-to-all-done = bf16[4,512,256]{2,0,1:T(4,128)(2,1)S(1)} async-done(((bf16[4,512,256]{2,0,1:T(4,128)(2,1)}), bf16[4,512,256]{2,0,1:T(4,128)(2,1)S(1)}, u32[]{:S(2)}, u32[]{:S(2)}) %all-to-all-start) | async-done | bytes 1048608 | tf_op jit(solution)/shard_map/all_to_all | solution.py:56
  47.1 0.2 copy.25
  47.3 0.0 copy-done.4
  47.3 0.5 fusion.34
  47.8 0.5 fusion.36
  48.3 0.0 copy-start.5
  48.3 1.1 fusion.3
  49.5 0.0 copy-done.5
  49.5 1.5 convolution_convert_fusion.2
  50.9 0.0 copy-start.6
  50.9 3.4 %reshape.53 = bf16[64,32,4,64]{3,2,1,0:T(4,128)(2,1)S(1)} reshape(bf16[64,32,256]{2,1,0:T(8,128)(2,1)} %convolution_convert_fusion.2) | data formatting | bytes 2097152 | tf_op jit(solution)/shard_map/reshape | solution.py:68
  54.3 0.0 copy-done.6
  54.3 1.5 convolution_convert_fusion.1
  55.8 0.0 copy-start.7
  55.8 4.5 %reshape.54 = bf16[64,32,4,64]{3,2,1,0:T(4,128)(2,1)} reshape(bf16[64,32,256]{2,1,0:T(8,128)(2,1)} %convolution_convert_fusion.1) | data formatting | bytes 2097152 | tf_op jit(solution)/shard_map/reshape | solution.py:69
  60.2 0.0 copy-done.7
  60.2 1.5 convolution_convert_fusion
  61.7 4.4 %reshape.55 = bf16[64,32,4,64]{3,2,1,0:T(4,128)(2,1)} reshape(bf16[64,32,256]{2,1,0:T(8,128)(2,1)} %convolution_convert_fusion) | data formatting | bytes 2097152 | tf_op jit(solution)/shard_map/reshape | solution.py:70
  66.1 4.1 %fusion.9 = f32[32,4,64,64]{2,3,1,0:T(8,128)S(1)} fusion(bf16[64,32,4,64]{3,2,1,0:T(4,128)(2,1)} %reshape.54, bf16[64,32,4,64]{3,2,1,0:T(4,128)(2,1)S(1)} %reshape.53), kind=kOutput, calls=%fused_computation.17 | convolution fusion | flops 67108864 | bytes 4194304 | tf_op jit(solution)/shard_map/qnhd,knhd->nhqk/dot_general | solution.py:71
  70.3 0.0 copy-start.2
  70.3 1.9 %fusion.44 = (f32[32,4,64]{2,1,0:T(4,128)S(1)}, bf16[32,4,64,64]{2,3,1,0:T(8,128)(2,1)S(1)}) fusion(f32[32,4,64,64]{2,3,1,0:T(8,128)S(1)} %fusion.9, pred[64]{0:T(512)(128)(4,1)S(1)} %get-tuple-element.10), kind=kOutput, calls=%fused_computation.54 | output fusion | flops 4194367 | bytes 3178560 | tf_op jit(solution)/shard_map/sub | solution.py:77
  72.2 0.0 copy-done.2
  72.2 3.3 %fusion.1 = bf16[64,32,4,64]{3,0,2,1:T(8,128)(2,1)S(1)} fusion(bf16[64,32,4,64]{3,2,1,0:T(4,128)(2,1)S(1)} %copy-done.2, f32[64,32,4]{0,2,1:T(4,128)S(1)} %bitcast.71, bf16[32,4,64,64]{2,3,1,0:T(8,128)(2,1)S(1)} %get-tuple-element.7), kind=kOutput, calls=%fused_computation.2 | convolution fusion | flops 68157440 | bytes 3178496 | tf_op jit(solution)/shard_map/nhqk,knhd->nhqd/dot_general | solution.py:79
  75.4 1.6 copy.30
  77.1 2.2 %reshape.56 = bf16[64,32,256]{2,1,0:T(8,128)(2,1)} reshape(bf16[64,32,4,64]{3,2,1,0:T(4,128)(2,1)S(1)} %copy.30) | data formatting | bytes 2097152 | tf_op jit(solution)/shard_map/reshape | solution.py:83
  79.2 0.0 copy-done
  79.2 3.5 %multiply_reduce_fusion = (f32[]{:T(128)}, bf16[64,32,256]{2,1,0:T(8,128)(2,1)}) fusion(f32[64]{0:T(128)S(1)} %get-tuple-element.11, bf16[64,32,256]{2,1,0:T(8,128)(2,1)} %reshape.56, bf16[256,256]{1,0:T(8,128)(2,1)S(1)} %copy-done, bf16[64,32,256]{2,1,0:T(8,128)(2,1)S(1)} %get-tuple-element.5), kind=kOutput, calls=%fused_computation.20 | convolution fusion | flops 272105472 | bytes 3277060 | tf_op jit(solution)/shard_map/tnc,oc->tno/dot_general | solution.py:31
  82.7 4.2 %all-to-all-start.1 = ((bf16[64,32,256]{2,1,0:T(8,128)(2,1)}), bf16[64,32,256]{2,1,0:T(8,128)(2,1)S(1)}, u32[]{:S(2)}, u32[]{:S(2)}) async-start(bf16[64,32,256]{2,1,0:T(8,128)(2,1)} %get-tuple-element.9), calls=%async_computation.1 | async-start | bytes 2097152 | tf_op jit(solution)/shard_map/all_to_all | solution.py:90
  86.9 72.7 %psum.7 = f32[]{:T(128)} all-reduce(f32[]{:T(128)} %get-tuple-element.8), channel_id=1, replica_groups=mesh['scene'=8,'frame'=16] {'scene','frame'}, use_global_device_ids=true, to_apply=%region_4.5 | all-reduce | flops 1 | bytes 8 | tf_op jit(solution)/shard_map/psum | solution.py:87
  160.2 0.0 all-to-all-done.1
  160.2 0.1 copy.31
  160.3 1.3 copy.32
  (3 shorter events, 0.0 us)
Async XLA Ops:
  0.6 78.6 %copy-start = (bf16[256,256]{1,0:T(8,128)(2,1)S(1)}, bf16[256,256]{1,0:T(8,128)(2,1)}, u32[]{:S(2)}) copy-start(bf16[256,256]{1,0:T(8,128)(2,1)} %param.17) | copy-start | bytes 393220
  4.0 2.9 %copy-start.3 = (bf16[1,4,64,2048]{3,2,1,0:T(8,128)(2,1)S(1)}, bf16[1,4,64,2048]{3,2,1,0:T(8,128)(2,1)}, u32[]{:S(2)}) copy-start(bf16[1,4,64,2048]{3,2,1,0:T(8,128)(2,1)} %param.9) | copy-start | bytes 3145732
  9.4 5.0 %copy-start.1 = (bf16[256,128,3,3,3]{0,4,3,2,1:T(4,128)(2,1)S(1)}, bf16[256,128,3,3,3]{0,4,3,2,1:T(4,128)(2,1)}, u32[]{:S(2)}) copy-start(bf16[256,128,3,3,3]{0,4,3,2,1:T(4,128)(2,1)} %reshape.51) | copy-start | bytes 5308420
  22.6 24.8 %copy-start.4 = (bf16[3,256,256]{2,1,0:T(8,128)(2,1)S(1)}, bf16[3,256,256]{2,1,0:T(8,128)(2,1)}, u32[]{:S(2)}) copy-start(bf16[3,256,256]{2,1,0:T(8,128)(2,1)} %param.13) | copy-start | bytes 1179652
  22.6 24.6 %all-to-all-start = ((bf16[4,512,256]{2,0,1:T(4,128)(2,1)}), bf16[4,512,256]{2,0,1:T(4,128)(2,1)S(1)}, u32[]{:S(2)}, u32[]{:S(2)}) async-start(bf16[4,512,256]{2,0,1:T(4,128)(2,1)} %bitcast.3), calls=%async_computation | async-start | bytes 2097152 | tf_op jit(solution)/shard_map/all_to_all | solution.py:56
  48.3 1.2 copy-start.5
  50.9 3.4 %copy-start.6 = (bf16[256,256]{1,0:T(8,128)(2,1)S(1)}, bf16[256,256]{1,0:T(8,128)(2,1)}, u32[]{:S(2)}) copy-start(bf16[256,256]{1,0:T(8,128)(2,1)} %param.15) | copy-start | bytes 393220
  55.8 4.5 %copy-start.7 = (bf16[256,256]{1,0:T(8,128)(2,1)S(1)}, bf16[256,256]{1,0:T(8,128)(2,1)}, u32[]{:S(2)}) copy-start(bf16[256,256]{1,0:T(8,128)(2,1)} %param.16) | copy-start | bytes 393220
  70.3 1.9 %copy-start.2 = (bf16[64,32,4,64]{3,2,1,0:T(4,128)(2,1)S(1)}, bf16[64,32,4,64]{3,2,1,0:T(4,128)(2,1)}, u32[]{:S(2)}) copy-start(bf16[64,32,4,64]{3,2,1,0:T(4,128)(2,1)} %reshape.55) | copy-start | bytes 3145732
  82.7 77.5 %all-to-all-start.1 = ((bf16[64,32,256]{2,1,0:T(8,128)(2,1)}), bf16[64,32,256]{2,1,0:T(8,128)(2,1)S(1)}, u32[]{:S(2)}, u32[]{:S(2)}) async-start(bf16[64,32,256]{2,1,0:T(8,128)(2,1)} %get-tuple-element.9), calls=%async_computation.1 | async-start | bytes 2097152 | tf_op jit(solution)/shard_map/all_to_all | solution.py:90
where the time goes:
time: 163 us
  blocking collectives  72.7 us (45%)
  matrix products  28.9 us (18%)
  local copies, waits for them, and re-layouts  25.7 us (16%)
  waiting for transfers between devices  16 us (10%)
  starting transfers between devices  12.8 us (8%)
  other arithmetic  3.44 us (2%)
  between operations  3.32 us (2%)
    psum x1, blocking collectives, shards(): grand_total = lax.psum(squares, ('scene', 'frame'))  72.7 us
    all_to_all x1, waiting for transfers between devices, shards(): lax.all_to_all(second_maps.transpose(0, 2, 1), 'frame', 1, 0, tiled=True)  16 us
    conv_general_dilated x2, matrix products, spatial_conv(): lax.conv_general_dilated(voxels, kernel, (stride, stride, 1), ((1, 1), (1...  11.6 us
    dot_general x7, matrix products, mix(): jnp.einsum('tnc,oc->tno', maps, weight, preferred_element_type=jnp.float32)  9.93 us
    all_to_all x1, starting transfers between devices, shards(): lax.all_to_all(second_maps.transpose(0, 2, 1), 'frame', 1, 0, tiled=True)  8.57 us
    unnamed x19, local copies, waits for them, and re-layouts  5.05 us
    reshape x1, local copies, waits for them, and re-layouts, shards(): keys = mix(normed, key_weight).astype(jnp.bfloat16).reshape(split)  4.45 us
    reshape x1, local copies, waits for them, and re-layouts, shards(): values = mix(normed, value_weight).astype(jnp.bfloat16).reshape(split)  4.44 us
  transfers between devices with their start and end apart: 2, of which 1 were waited for; matrix products, arithmetic and copies ran while one was open for 0% of the time, Pallas kernels for 0%

commit v1 on v0

--- a/solution.py
+++ b/solution.py
@@ -53,7 +53,15 @@
     second_maps = (second_full.reshape(f_dev, C2, CELLS) * valid_rows[:, None, None]).astype(
         jnp.bfloat16
     )
-    second = lax.all_to_all(second_maps.transpose(0, 2, 1), "frame", 1, 0, tiled=True)
+    second = jnp.concatenate(
+        lax.all_to_all(
+            jnp.stack(jnp.split(second_maps.transpose(0, 2, 1), lax.axis_size("frame"), axis=1)),
+            "frame",
+            0,
+            0,
+        ),
+        axis=0,
+    )
     frames, cells = second.shape[:2]
     padded = jnp.pad(second, ((1, 1), (0, 0), (0, 0)))
     temporal_sum = mix(padded[0:frames], temporal_weight[0])

time: 163 us -> 173 us (1.061)
  local copies, waits for them, and re-layouts: 25.7 us -> 36.2 us
    unnamed x19 -> x34, local copies, waits for them, and re-layouts: 5.05 us -> 14.8 us
where the time goes in v1:
time: 173 us; the launch traced here: 172 us
  blocking collectives  72.7 us (42%)
  local copies, waits for them, and re-layouts  36.2 us (21%)
  matrix products  28.9 us (17%)
  waiting for transfers between devices  16 us (9%)
  starting transfers between devices  12.8 us (7%)
  between operations  3.33 us (2%)
  other arithmetic  2.47 us (1%)
    psum x1, blocking collectives, shards(): grand_total = lax.psum(squares, ('scene', 'frame'))  72.7 us
    all_to_all x1, waiting for transfers between devices, shards(): lax.all_to_all(jnp.stack(jnp.split(second_maps.transpose(0, 2, 1), lax.ax...  16 us
    unnamed x34, local copies, waits for them, and re-layouts  14.8 us
    conv_general_dilated x2, matrix products, spatial_conv(): lax.conv_general_dilated(voxels, kernel, (stride, stride, 1), ((1, 1), (1...  11.6 us
    dot_general x7, matrix products, mix(): jnp.einsum('tnc,oc->tno', maps, weight, preferred_element_type=jnp.float32)  9.93 us
    all_to_all x1, starting transfers between devices, shards(): lax.all_to_all(jnp.stack(jnp.split(second_maps.transpose(0, 2, 1), lax.ax...  8.57 us
    reshape x1, local copies, waits for them, and re-layouts, shards(): keys = mix(normed, key_weight).astype(jnp.bfloat16).reshape(split)  4.45 us
    reshape x1, local copies, waits for them, and re-layouts, shards(): values = mix(normed, value_weight).astype(jnp.bfloat16).reshape(split)  4.44 us
  transfers between devices with their start and end apart: 2, of which 1 were waited for; matrix products, arithmetic and copies ran while one was open for 0% of the time, Pallas kernels for 0%

profile of v1, /device:TPU:1, one launch (start us, length us, event | category | flops | bytes accessed | tf_op | source)
XLA Modules:
  0.0 172.3 jit_solution(8227732353783583039)
XLA Ops:
  0.6 0.0 copy-start
  1.3 2.6 %copy.23 = bf16[256,3456]{0,1:T(8,128)(2,1)S(1)} copy(bf16[256,3456]{1,0:T(8,128)(2,1)} %param.12) | data formatting | bytes 3538944 | tf_op args[3]
  4.0 0.0 copy-start.3
  4.0 2.9 %reshape.54 = bf16[256,128,3,3,3]{0,4,3,2,1:T(4,128)(2,1)} reshape(bf16[256,3456]{0,1:T(8,128)(2,1)S(1)} %copy.23) | data formatting | bytes 3538944 | tf_op jit(solution)/shard_map/reshape | solution.py:19
  6.8 0.0 copy-done.3
  6.8 1.1 copy.20
  7.9 1.5 reshape.53
  9.4 0.0 copy-start.1
  9.4 5.0 %fusion.22 = bf16[4,128,8,8,8]{1,0,4,3,2:T(4,128)(2,1)S(1)} fusion(bf16[4,64,16,16,8]{1,4,3,2,0:T(8,128)(2,1)S(1)} %bitcast.146, bf16[128,64,3,3,3]{0,4,3,2,1:T(4,128)(2,1)S(1)} %reshape.53), kind=kOutput, calls=%fused_computation.34 | convolution fusion | flops 764018688 | bytes 2015232 | tf_op jit(solution)/shard_map/conv_general_dilated | solution.py:20
  14.4 0.0 copy-done.1
  14.4 6.6 %divide_multiply_fusion = f32[4,256,8,8,8]{1,0,4,3,2:T(4,128)S(1)} fusion(bf16[4,128,8,8,8]{1,0,4,3,2:T(4,128)(2,1)S(1)} %fusion.22, bf16[256,128,3,3,3]{0,4,3,2,1:T(4,128)(2,1)S(1)} %copy-done.1), kind=kOutput, calls=%fused_computation.9 | convolution fusion | flops 2793406464 | bytes 4390912 | tf_op jit(solution)/shard_map/conv_general_dilated | solution.py:20
  21.0 0.6 fusion.7
  21.6 0.7 fusion.56
  22.3 0.7 fusion.55
  22.9 0.7 fusion.54
  23.6 0.7 fusion.53
  24.2 0.7 fusion.52
  24.9 0.7 fusion.51
  25.5 0.7 fusion.50
  26.2 0.7 fusion.49
  26.8 0.7 fusion.48
  27.5 0.7 fusion.47
  28.1 0.7 fusion.46
  28.8 0.7 fusion.45
  29.4 0.7 fusion.44
  30.1 0.7 fusion.43
  30.8 0.7 fusion.42
  31.4 0.7 fusion.41
  32.1 0.0 copy-start.4
  32.1 8.6 %all-to-all-start = ((bf16[16,4,32,256]{3,1,2,0:T(4,128)(2,1)}), bf16[16,4,32,256]{3,1,2,0:T(4,128)(2,1)S(1)}, u32[]{:S(2)}, u32[]{:S(2)}) async-start(bf16[16,4,32,256]{3,1,2,0:T(4,128)(2,1)} %fusion.41), calls=%async_computation | async-start | bytes 2097152 | tf_op jit(solution)/shard_map/all_to_all | solution.py:57
  40.7 16.0 %all-to-all-done = bf16[16,4,32,256]{3,1,2,0:T(4,128)(2,1)S(1)} async-done(((bf16[16,4,32,256]{3,1,2,0:T(4,128)(2,1)}), bf16[16,4,32,256]{3,1,2,0:T(4,128)(2,1)S(1)}, u32[]{:S(2)}, u32[]{:S(2)}) %all-to-all-start) | async-done | bytes 1048608 | tf_op jit(solution)/shard_map/all_to_all | solution.py:57
  56.6 0.2 copy.25
  56.8 0.0 copy-done.4
  56.8 0.5 fusion.34
  57.3 0.5 fusion.36
  57.8 0.0 copy-start.5
  57.8 1.1 fusion.3
  59.0 0.0 copy-done.5
  59.0 1.5 convolution_convert_fusion.2
  60.4 0.0 copy-start.6
  60.4 3.4 %reshape.57 = bf16[64,32,4,64]{3,2,1,0:T(4,128)(2,1)S(1)} reshape(bf16[64,32,256]{2,1,0:T(8,128)(2,1)} %convolution_convert_fusion.2) | data formatting | bytes 2097152 | tf_op jit(solution)/shard_map/reshape | solution.py:76
  63.8 0.0 copy-done.6
  63.8 1.5 convolution_convert_fusion.1
  65.3 0.0 copy-start.7
  65.3 4.5 %reshape.58 = bf16[64,32,4,64]{3,2,1,0:T(4,128)(2,1)} reshape(bf16[64,32,256]{2,1,0:T(8,128)(2,1)} %convolution_convert_fusion.1) | data formatting | bytes 2097152 | tf_op jit(solution)/shard_map/reshape | solution.py:77
  69.7 0.0 copy-done.7
  69.7 1.5 convolution_convert_fusion
  71.2 4.4 %reshape.59 = bf16[64,32,4,64]{3,2,1,0:T(4,128)(2,1)} reshape(bf16[64,32,256]{2,1,0:T(8,128)(2,1)} %convolution_convert_fusion) | data formatting | bytes 2097152 | tf_op jit(solution)/shard_map/reshape | solution.py:78
  75.6 4.1 %fusion.9 = f32[32,4,64,64]{2,3,1,0:T(8,128)S(1)} fusion(bf16[64,32,4,64]{3,2,1,0:T(4,128)(2,1)} %reshape.58, bf16[64,32,4,64]{3,2,1,0:T(4,128)(2,1)S(1)} %reshape.57), kind=kOutput, calls=%fused_computation.17 | convolution fusion | flops 67108864 | bytes 4194304 | tf_op jit(solution)/shard_map/qnhd,knhd->nhqk/dot_general | solution.py:79
  79.8 0.0 copy-start.2
  79.8 1.9 %fusion.60 = (f32[32,4,64]{2,1,0:T(4,128)S(1)}, bf16[32,4,64,64]{2,3,1,0:T(8,128)(2,1)S(1)}) fusion(f32[32,4,64,64]{2,3,1,0:T(8,128)S(1)} %fusion.9, pred[64]{0:T(512)(128)(4,1)S(1)} %get-tuple-element.10), kind=kOutput, calls=%fused_computation.86 | output fusion | flops 4194367 | bytes 3178560 | tf_op jit(solution)/shard_map/sub | solution.py:85
  81.6 0.0 copy-done.2
  81.7 3.3 %fusion.1 = bf16[64,32,4,64]{3,0,2,1:T(8,128)(2,1)S(1)} fusion(bf16[64,32,4,64]{3,2,1,0:T(4,128)(2,1)S(1)} %copy-done.2, f32[64,32,4]{0,2,1:T(4,128)S(1)} %bitcast.147, bf16[32,4,64,64]{2,3,1,0:T(8,128)(2,1)S(1)} %get-tuple-element.7), kind=kOutput, calls=%fused_computation.2 | convolution fusion | flops 68157440 | bytes 3178496 | tf_op jit(solution)/shard_map/nhqk,knhd->nhqd/dot_general | solution.py:87
  84.9 1.6 copy.30
  86.6 2.2 %reshape.60 = bf16[64,32,256]{2,1,0:T(8,128)(2,1)} reshape(bf16[64,32,4,64]{3,2,1,0:T(4,128)(2,1)S(1)} %copy.30) | data formatting | bytes 2097152 | tf_op jit(solution)/shard_map/reshape | solution.py:91
  88.7 0.0 copy-done
  88.7 3.5 %multiply_reduce_fusion = (f32[]{:T(128)}, bf16[64,32,256]{2,1,0:T(8,128)(2,1)}) fusion(f32[64]{0:T(128)S(1)} %get-tuple-element.11, bf16[64,32,256]{2,1,0:T(8,128)(2,1)} %reshape.60, bf16[256,256]{1,0:T(8,128)(2,1)S(1)} %copy-done, bf16[64,32,256]{2,1,0:T(8,128)(2,1)S(1)} %get-tuple-element.5), kind=kOutput, calls=%fused_computation.20 | convolution fusion | flops 272105472 | bytes 3277060 | tf_op jit(solution)/shard_map/tnc,oc->tno/dot_general | solution.py:31
  92.2 4.2 %all-to-all-start.1 = ((bf16[64,32,256]{2,1,0:T(8,128)(2,1)}), bf16[64,32,256]{2,1,0:T(8,128)(2,1)S(1)}, u32[]{:S(2)}, u32[]{:S(2)}) async-start(bf16[64,32,256]{2,1,0:T(8,128)(2,1)} %get-tuple-element.9), calls=%async_computation.1 | async-start | bytes 2097152 | tf_op jit(solution)/shard_map/all_to_all | solution.py:98
  96.4 72.7 %psum.7 = f32[]{:T(128)} all-reduce(f32[]{:T(128)} %get-tuple-element.8), channel_id=1, replica_groups=mesh['scene'=8,'frame'=16] {'scene','frame'}, use_global_device_ids=true, to_apply=%region_4.5 | all-reduce | flops 1 | bytes 8 | tf_op jit(solution)/shard_map/psum | solution.py:95
  169.7 0.0 all-to-all-done.1
  169.7 0.1 copy.31
  169.8 1.3 copy.32
  (3 shorter events, 0.0 us)
Async XLA Ops:
  0.6 88.1 %copy-start = (bf16[256,256]{1,0:T(8,128)(2,1)S(1)}, bf16[256,256]{1,0:T(8,128)(2,1)}, u32[]{:S(2)}) copy-start(bf16[256,256]{1,0:T(8,128)(2,1)} %param.17) | copy-start | bytes 393220
  4.0 2.9 %copy-start.3 = (bf16[1,4,64,2048]{3,2,1,0:T(8,128)(2,1)S(1)}, bf16[1,4,64,2048]{3,2,1,0:T(8,128)(2,1)}, u32[]{:S(2)}) copy-start(bf16[1,4,64,2048]{3,2,1,0:T(8,128)(2,1)} %param.9) | copy-start | bytes 3145732
  9.4 5.0 %copy-start.1 = (bf16[256,128,3,3,3]{0,4,3,2,1:T(4,128)(2,1)S(1)}, bf16[256,128,3,3,3]{0,4,3,2,1:T(4,128)(2,1)}, u32[]{:S(2)}) copy-start(bf16[256,128,3,3,3]{0,4,3,2,1:T(4,128)(2,1)} %reshape.54) | copy-start | bytes 5308420
  32.1 24.8 %copy-start.4 = (bf16[3,256,256]{2,1,0:T(8,128)(2,1)S(1)}, bf16[3,256,256]{2,1,0:T(8,128)(2,1)}, u32[]{:S(2)}) copy-start(bf16[3,256,256]{2,1,0:T(8,128)(2,1)} %param.13) | copy-start | bytes 1179652
  32.1 24.6 %all-to-all-start = ((bf16[16,4,32,256]{3,1,2,0:T(4,128)(2,1)}), bf16[16,4,32,256]{3,1,2,0:T(4,128)(2,1)S(1)}, u32[]{:S(2)}, u32[]{:S(2)}) async-start(bf16[16,4,32,256]{3,1,2,0:T(4,128)(2,1)} %fusion.41), calls=%async_computation | async-start | bytes 2097152 | tf_op jit(solution)/shard_map/all_to_all | solution.py:57
  57.8 1.2 copy-start.5
  60.4 3.4 %copy-start.6 = (bf16[256,256]{1,0:T(8,128)(2,1)S(1)}, bf16[256,256]{1,0:T(8,128)(2,1)}, u32[]{:S(2)}) copy-start(bf16[256,256]{1,0:T(8,128)(2,1)} %param.15) | copy-start | bytes 393220
  65.3 4.5 %copy-start.7 = (bf16[256,256]{1,0:T(8,128)(2,1)S(1)}, bf16[256,256]{1,0:T(8,128)(2,1)}, u32[]{:S(2)}) copy-start(bf16[256,256]{1,0:T(8,128)(2,1)} %param.16) | copy-start | bytes 393220
  79.8 1.9 %copy-start.2 = (bf16[64,32,4,64]{3,2,1,0:T(4,128)(2,1)S(1)}, bf16[64,32,4,64]{3,2,1,0:T(4,128)(2,1)}, u32[]{:S(2)}) copy-start(bf16[64,32,4,64]{3,2,1,0:T(4,128)(2,1)} %reshape.59) | copy-start | bytes 3145732
  92.2 77.5 %all-to-all-start.1 = ((bf16[64,32,256]{2,1,0:T(8,128)(2,1)}), bf16[64,32,256]{2,1,0:T(8,128)(2,1)S(1)}, u32[]{:S(2)}, u32[]{:S(2)}) async-start(bf16[64,32,256]{2,1,0:T(8,128)(2,1)} %get-tuple-element.9), calls=%async_computation.1 | async-start | bytes 2097152 | tf_op jit(solution)/shard_map/all_to_all | solution.py:98
